TPU v7x, 32 devices: a whole 2x2x4 slice. The times are simulated.
32 devices in a mesh: chan: 8 (over z, x), tile: 4 (over y, core).
Axes of the slice: x: 2, y: 2, z: 4, core: 2. Of those that a mesh axis runs over, the one named last changes fastest.
Arguments:
- voltages: bfloat16 [2, 1024, 5888], P(None, 'chan'), may hold values from -6 to 6
- taps: float32 [16, 256], replicated, may hold values from -0.09375 to 0.09375
- beam_weights: bfloat16 [2, 256, 64, 1024], P(None, 'chan'), may hold values from -0.1875 to 0.1875
- station_masks: int32 [64, 512], replicated, may hold values 0 or 1
- tile_pairs: int32 [36, 2], P('tile'), may hold values from 0 to 7, as said below
Outputs:
- visibilities: float32 [2, 256, 36, 128, 128], P(None, 'chan', 'tile')
- beams: bfloat16 [2, 64, 8, 256], P(None, 'tile', 'chan')
Inputs may be any that keep to these rules, and one draw needn't show every extreme that they name: `tile_pairs`: each pair (r, s) with 0 <= s <= r < 8 stands in exactly one row, r in the first column and s in the second.
All inputs are finite; a program needn't handle non-finite values.
Results may differ from a plain program's by a relative error of at most 0.0049.
Values may be sent and summed in bfloat16 or wider, within the bound.
A program may use at most 128 MiB of HBM per device.

v0:
```python
import math
import jax
import jax.numpy as jnp
from jax import lax
from jax.sharding import PartitionSpec as P

TB = 128


def dft_table(channels):
    counter = jnp.arange(channels, dtype=jnp.int32)
    wrapped = counter[:, None] * counter[None, :] % channels
    phases = 2.0 * math.pi / channels * wrapped.astype(jnp.float32)
    cosine = jnp.cos(phases)
    sine_part = jnp.sin(phases)
    first_row = jnp.stack([cosine, sine_part], axis=1)
    second_row = jnp.stack([-sine_part, cosine], axis=1)
    return jnp.stack([first_row, second_row], axis=1)


def filterbank(voltages, taps, count):
    taps_count, channels = taps.shape
    in_dev = voltages.shape[1]
    framed = voltages.reshape(2, in_dev, count + taps_count - 1, channels)
    frames = jnp.zeros((2, in_dev, count, channels), jnp.float32)
    for tap_index in range(taps_count):
        frames = frames + taps[tap_index] * framed[:, :, tap_index : tap_index + count, :].astype(
            jnp.float32
        )
    spectra = jnp.einsum(
        "crsk,sitk->crit",
        dft_table(channels),
        frames,
        precision=lax.Precision.HIGHEST,
        preferred_element_type=jnp.float32,
    )
    return spectra.astype(jnp.bfloat16)


def correlate(time_piece, tile_pairs):
    chan_dev = time_piece.shape[0]
    inputs = time_piece.shape[2]
    time_width = time_piece.shape[3]
    blocks = time_piece.reshape(chan_dev, 2, inputs // TB, TB, time_width)
    left_rows = jnp.take(blocks, tile_pairs[:, 0], axis=2)
    right_rows = jnp.take(blocks, tile_pairs[:, 1], axis=2)
    rotated = jnp.stack([left_rows[:, 1], -left_rows[:, 0]], axis=1)
    stacked = jnp.stack([left_rows, rotated], axis=0)
    return jnp.einsum(
        "ocrkaw,crkbw->ockab", stacked, right_rows, preferred_element_type=jnp.float32
    )


def beamform(own_time, beam_weights, station_masks):
    beams_count, stations = station_masks.shape
    live_inputs = jnp.broadcast_to(station_masks[:, :, None], (beams_count, stations, 2))
    live_inputs = live_inputs.reshape(beams_count, 2 * stations).astype(jnp.bfloat16)
    weights = beam_weights * live_inputs[None, None]
    products = jnp.einsum("scbi,crit->csrbt", weights, own_time, preferred_element_type=jnp.float32)
    real_part = products[:, 0, 0] - products[:, 1, 1]
    imag_part = products[:, 0, 1] + products[:, 1, 0]
    return jnp.transpose(jnp.stack([real_part, imag_part]), (0, 2, 3, 1)).astype(jnp.bfloat16)


def on_device(voltages, taps, beam_weights, station_masks, tile_pairs):
    taps_count, channels = taps.shape
    tile_count = lax.axis_size("tile")
    total_time = voltages.shape[2] // channels - taps_count + 1
    quarter = total_time // tile_count
    tile_index = lax.axis_index("tile")
    spectra = filterbank(voltages, taps, total_time)
    turned = lax.all_to_all(spectra, "chan", split_axis=0, concat_axis=2, tiled=True)
    own_time = lax.dynamic_slice_in_dim(turned, tile_index * quarter, quarter, 3)
    visibility = correlate(turned, tile_pairs)
    visibility = visibility * (1.0 / total_time)
    beam_part = beamform(own_time, beam_weights, station_masks)
    beams = lax.all_to_all(
        lax.all_to_all(beam_part, "tile", split_axis=1, concat_axis=2, tiled=True),
        "chan",
        split_axis=2,
        concat_axis=3,
        tiled=True,
    )
    return (visibility, beams)


def solution(mesh):
    in_specs = (P(None, "chan", None), P(), P(None, "chan", None, None), P(), P("tile", None))
    out_specs = (P(None, "chan", "tile", None, None), P(None, "tile", "chan", None))
    return jax.shard_map(
        on_device, mesh=mesh, in_specs=in_specs, out_specs=out_specs, check_vma=False
    )
```

profile of v0, /device:TPU:0, one launch (start us, length us, event | category | flops | bytes accessed | tf_op | source)
XLA Modules:
  0.0 124.9 jit_solution(12216933234083120169)
XLA Ops:
  0.6 1.0 fusion.109
  1.6 1.7 %fusion.107 = (f32[256,1,256]{2,0,1:T(8,128)S(1)}, f32[256,1,256]{2,0,1:T(8,128)}) fusion(), kind=kLoop, calls=%fused_computation.119 | loop fusion | flops 917504 | bytes 524288 | tf_op jit(solution)/shard_map/sin | solution.py:15
  3.3 1.7 %fusion.119 = (f32[1,256]{1,0:T(1,128)S(1)}, f32[1,256]{1,0:T(1,128)S(1)}, f32[1,256]{1,0:T(1,128)S(1)}, f32[1,256]{1,0:T(1,128)S(1)}, f32[1,256]{1,0:T(1,128)},...) fusion(f32[16,256]{1,0:T(8,128)} %param.8), kind=kLoop, calls=%fused_computation.141 | loop fusion | bytes 32768 | tf_op jit(solution)/shard_map/slice | solution.py:27
  5.0 3.5 %copy.96 = bf16[2,128,5888]{1,2,0:T(8,128)(2,1)S(1)} copy(bf16[2,128,5888]{2,1,0:T(8,128)(2,1)} %param.7) | data formatting | bytes 6029312 | tf_op args[0]
  8.5 1.1 maximum_bitcast_fusion.1
  9.6 7.1 %bitcast_convert_fusion = bf16[256,2,128,8]{2,0,3,1:T(8,128)(2,1)S(1)} fusion(bf16[2,128,23,256]{1,3,2,0:T(8,128)(2,1)S(1)} %bitcast.122, f32[256,1,2,256]{3,0,2,1:T(8,128)S(1)} %get-tuple-element.26, f32[256,1,2,256]{3,0,2,1:T(8,128)S(1)} %get-tuple-element.25, f32[256]{0:T(256)} %bitcast.145, f32[256]{0:T(256)} %bitcast.146, f32[256]{0:T(256)S(1)} %bitcast.132, ...), kind=kOutput, calls=%fused_computation.10 | convolution fusion | flops 3246653440 | bytes 18890752 | tf_op jit(solution)/shard_map/crsk,sitk->crit/dot_general | solution.py:30
  16.7 0.0 copy-start
  16.7 1.6 %copy.98 = bf16[256,2,128,8]{2,3,1,0:T(8,128)(2,1)} copy(bf16[256,2,128,8]{2,0,3,1:T(8,128)(2,1)S(1)} %bitcast_convert_fusion) | data formatting | bytes 2097152 | tf_op jit(solution)/shard_map/convert_element_type | solution.py:37
  18.4 7.4 %all-to-all-start = ((bf16[256,2,128,8]{2,3,1,0:T(8,128)(2,1)}), bf16[256,2,128,8]{2,3,1,0:T(8,128)(2,1)S(1)}, u32[]{:S(2)}, u32[]{:S(2)}) async-start(bf16[256,2,128,8]{2,3,1,0:T(8,128)(2,1)} %copy.98), calls=%async_computation | async-start | bytes 2097152 | tf_op jit(solution)/shard_map/all_to_all | solution.py:72
  25.8 0.1 copy.103
  25.9 0.1 broadcast_in_dim.11
  26.1 0.1 copy.104
  26.2 25.3 %all-to-all-done = bf16[256,2,128,8]{2,3,1,0:T(8,128)(2,1)S(1)} async-done(((bf16[256,2,128,8]{2,3,1,0:T(8,128)(2,1)}), bf16[256,2,128,8]{2,3,1,0:T(8,128)(2,1)S(1)}, u32[]{:S(2)}, u32[]{:S(2)}) %all-to-all-start) | async-done | bytes 1048608 | tf_op jit(solution)/shard_map/all_to_all | solution.py:72
  51.5 0.3 copy.144
  51.8 6.9 %fusion.58 = f32[32,2,2,64,2]{3,4,1,2,0:T(2,128)S(1)} fusion(bf16[32,2,1024,8]{2,3,1,0:T(8,128)(2,1)S(1)} %bitcast.118, s32[]{:T(128)S(6)} %select_n.39, bf16[2,32,64,1024]{3,2,1,0:T(8,128)(2,1)} %param.9, bf16[64,1024]{1,0:T(8,128)(2,1)S(1)} %copy.104), kind=kOutput, calls=%fused_computation.64 | convolution fusion | flops 37748736 | bytes 8847364 | tf_op jit(solution)/shard_map/scbi,crit->csrbt/dot_general | solution.py:59
  58.7 0.1 maximum_bitcast_fusion.3
  58.8 0.1 copy.108
  58.9 0.7 reshape.184
  59.7 3.3 %all-to-all-start.1 = ((bf16[4,2,1024]{2,1,0:T(2,128)(2,1)}), bf16[4,2,1024]{2,1,0:T(2,128)(2,1)S(1)}, u32[]{:S(2)}, u32[]{:S(2)}) async-start(bf16[4,2,1024]{2,1,0:T(2,128)(2,1)} %reshape.184), calls=%async_computation.1 | async-start | bytes 32768 | tf_op jit(solution)/shard_map/all_to_all | solution.py:78
  62.9 1.0 gather_fusion.1
  63.9 1.2 fusion.97
  65.1 0.2 fusion.118
  65.3 0.2 maximum_bitcast_fusion
  65.5 1.0 gather_fusion
  66.5 0.2 all-to-all-done.1
  66.7 0.1 reshape.185
  66.9 0.7 reshape.186
  67.6 3.6 %all-to-all-start.2 = ((bf16[8,2,512]{2,1,0:T(2,128)(2,1)}), bf16[8,2,512]{2,1,0:T(2,128)(2,1)S(1)}, u32[]{:S(2)}, u32[]{:S(2)}) async-start(bf16[8,2,512]{2,1,0:T(2,128)(2,1)} %reshape.186), calls=%async_computation.2 | async-start | bytes 32768 | tf_op jit(solution)/shard_map/all_to_all | solution.py:77
  71.2 16.0 %fusion = f32[2,32,9,128,128]{3,4,0,2,1:T(8,128)} fusion(bf16[1,32,2,9,128,8]{4,5,2,0,3,1:T(8,128)(2,1)S(1)} %maximum_bitcast_fusion, bf16[1,32,2,9,128,8]{4,5,2,0,3,1:T(8,128)(2,1)} %get-tuple-element.19, bf16[9,32,2,128,8]{3,4,2,1,0:T(8,128)(2,1)S(1)} %gather_fusion, pred[9]{0:T(512)(128)(4,1)S(1)} %get-tuple-element.15), kind=kOutput, calls=%fused_computation.3 | convolution fusion | flops 316735488 | bytes 41287688 | tf_op jit(solution)/shard_map/ocrkaw,crkbw->ockab/dot_general | solution.py:49
  87.2 36.9 %copy.113 = f32[2,32,9,128,128]{4,3,2,1,0:T(8,128)} copy(f32[2,32,9,128,128]{3,4,0,2,1:T(8,128)} %fusion) | data formatting | bytes 75497472
  124.1 0.1 reshape.187
  124.2 0.7 all_to_all.44
  (13 shorter events, 0.1 us)
Async XLA Ops:
  16.7 9.1 %copy-start = (s32[64,512]{1,0:T(8,128)S(1)}, s32[64,512]{1,0:T(8,128)}, u32[]{:S(2)}) copy-start(s32[64,512]{1,0:T(8,128)} %param.10) | copy-start | bytes 393220
  18.4 7.8 %copy-start.1 = (s32[9,2]{0,1:T(2,128)S(1)}, s32[9,2]{0,1:T(2,128)}, u32[]{:S(2)}) copy-start(s32[9,2]{0,1:T(2,128)} %param.11) | copy-start | bytes 220
  18.4 33.2 %all-to-all-start = ((bf16[256,2,128,8]{2,3,1,0:T(8,128)(2,1)}), bf16[256,2,128,8]{2,3,1,0:T(8,128)(2,1)S(1)}, u32[]{:S(2)}, u32[]{:S(2)}) async-start(bf16[256,2,128,8]{2,3,1,0:T(8,128)(2,1)} %copy.98), calls=%async_computation | async-start | bytes 2097152 | tf_op jit(solution)/shard_map/all_to_all | solution.py:72
  59.7 7.1 %all-to-all-start.1 = ((bf16[4,2,1024]{2,1,0:T(2,128)(2,1)}), bf16[4,2,1024]{2,1,0:T(2,128)(2,1)S(1)}, u32[]{:S(2)}, u32[]{:S(2)}) async-start(bf16[4,2,1024]{2,1,0:T(2,128)(2,1)} %reshape.184), calls=%async_computation.1 | async-start | bytes 32768 | tf_op jit(solution)/shard_map/all_to_all | solution.py:78
  67.6 56.5 %all-to-all-start.2 = ((bf16[8,2,512]{2,1,0:T(2,128)(2,1)}), bf16[8,2,512]{2,1,0:T(2,128)(2,1)S(1)}, u32[]{:S(2)}, u32[]{:S(2)}) async-start(bf16[8,2,512]{2,1,0:T(2,128)(2,1)} %reshape.186), calls=%async_computation.2 | async-start | bytes 32768 | tf_op jit(solution)/shard_map/all_to_all | solution.py:77
where the time goes:
time: 126 us; the launch traced here: 125 us
  local copies, waits for them, and re-layouts  48.9 us (39%)
  matrix products  29.9 us (24%)
  waiting for transfers between devices  25.5 us (20%)
  starting transfers between devices  14.2 us (11%)
  other arithmetic  5.54 us (4%)
    unnamed x10, local copies, waits for them, and re-layouts  42 us
    all_to_all x1, waiting for transfers between devices, on_device(): lax.all_to_all(spectra, 'chan', split_axis=0, concat_axis=2, tiled=True)  25.3 us
    dot_general x1, matrix products, correlate(): jnp.einsum('ocrkaw,crkbw->ockab', stacked, right_rows, preferred_element_...  16 us
    all_to_all x1, starting transfers between devices, on_device(): lax.all_to_all(spectra, 'chan', split_axis=0, concat_axis=2, tiled=True)  7.38 us
    dot_general x1, matrix products, filterbank(): jnp.einsum('crsk,sitk->crit', dft_table(channels), frames, precision=lax....  7.12 us
    dot_general x1, matrix products, beamform(): jnp.einsum('scbi,crit->csrbt', weights, own_time, preferred_element_type=...  6.86 us
    all_to_all x1, starting transfers between devices, on_device(): lax.all_to_all(lax.all_to_all(beam_part, 'tile', split_axis=1, concat_axi...  3.59 us
    all_to_all x1, starting transfers between devices, on_device(): lax.all_to_all(beam_part, 'tile', split_axis=1, concat_axis=2, tiled=True)  3.25 us
  transfers between devices with their start and end apart: 3, of which 2 were waited for; matrix products, arithmetic and copies ran while one was open for 46% of the time, Pallas kernels for 0%

commit v1 on v0

--- a/solution.py
+++ b/solution.py
@@ -5,6 +5,22 @@
 from jax.sharding import PartitionSpec as P
 
 TB = 128
+
+
+def pairwise_exchange(x, axis, split, join):
+    ways, here = (lax.axis_size(axis), lax.axis_index(axis))
+    width = x.shape[split] // ways
+    dims = list(x.shape)
+    dims[split] = width
+    height = dims[join]
+    dims[join] = height * ways
+    full = jnp.zeros(dims, x.dtype)
+    for mask in range(ways):
+        part = lax.dynamic_slice_in_dim(x, (here ^ mask) * width, width, axis=split)
+        if mask:
+            part = lax.ppermute(part, axis, [(d, d ^ mask) for d in range(ways)])
+        full = lax.dynamic_update_slice_in_dim(full, part, (here ^ mask) * height, axis=join)
+    return full
 
 
 def dft_table(channels):
@@ -69,7 +85,7 @@
     quarter = total_time // tile_count
     tile_index = lax.axis_index("tile")
     spectra = filterbank(voltages, taps, total_time)
-    turned = lax.all_to_all(spectra, "chan", split_axis=0, concat_axis=2, tiled=True)
+    turned = pairwise_exchange(spectra, "chan", 0, 2)
     own_time = lax.dynamic_slice_in_dim(turned, tile_index * quarter, quarter, 3)
     visibility = correlate(turned, tile_pairs)
     visibility = visibility * (1.0 / total_time)

time: 126 us -> 122 us (0.968)
  waiting for transfers between devices: 25.5 us -> 12.5 us
  starting transfers between devices: 14.2 us -> 24.5 us
    all_to_all x1 -> x0, waiting for transfers between devices: 25.3 us -> none  [on_device(): lax.all_to_all(spectra, 'chan', split_axis=0, concat_axis=2, tiled=True)]
    ppermute x0 -> x7, starting transfers between devices: none -> 17.1 us  [pairwise_exchange(): part = lax.ppermute(part, axis, [(d, d ^ mask) for d in range(ways)])]
    ppermute x0 -> x7, waiting for transfers between devices: none -> 12.4 us  [pairwise_exchange(): part = lax.ppermute(part, axis, [(d, d ^ mask) for d in range(ways)])]
    all_to_all x1 -> x0, starting transfers between devices: 7.38 us -> none  [on_device(): lax.all_to_all(spectra, 'chan', split_axis=0, concat_axis=2, tiled=True)]
    convert_element_type x1 -> x0, local copies, waits for them, and re-layouts: 1.65 us -> none  [filterbank(): return spectra.astype(jnp.bfloat16)]
  transfers between devices with their start and end apart: 3 -> 9, of which waited for: 2 -> 4; matrix products, arithmetic and copies ran while one was open for 46% -> 47% of each run, Pallas kernels for 0% -> 0%
where the time goes in v1:
time: 122 us; the launch traced here: 121 us
  local copies, waits for them, and re-layouts  47.8 us (39%)
  matrix products  29.9 us (25%)
  starting transfers between devices  24.5 us (20%)
  waiting for transfers between devices  12.5 us (10%)
  other arithmetic  5.55 us (5%)
    unnamed x10, local copies, waits for them, and re-layouts  42 us
    ppermute x7, starting transfers between devices, pairwise_exchange(): part = lax.ppermute(part, axis, [(d, d ^ mask) for d in range(ways)])  17.1 us
    dot_general x1, matrix products, correlate(): jnp.einsum('ocrkaw,crkbw->ockab', stacked, right_rows, preferred_element_...  16 us
    ppermute x7, waiting for transfers between devices, pairwise_exchange(): part = lax.ppermute(part, axis, [(d, d ^ mask) for d in range(ways)])  12.4 us
    dot_general x1, matrix products, filterbank(): jnp.einsum('crsk,sitk->crit', dft_table(channels), frames, precision=lax....  7.13 us
    dot_general x1, matrix products, beamform(): jnp.einsum('scbi,crit->csrbt', weights, own_time, preferred_element_type=...  6.84 us
    all_to_all x1, starting transfers between devices, on_device(): lax.all_to_all(lax.all_to_all(beam_part, 'tile', split_axis=1, concat_axi...  3.97 us
    all_to_all x1, starting transfers between devices, on_device(): lax.all_to_all(beam_part, 'tile', split_axis=1, concat_axis=2, tiled=True)  3.43 us
  transfers between devices with their start and end apart: 9, of which 4 were waited for; matrix products, arithmetic and copies ran while one was open for 47% of the time, Pallas kernels for 0%

profile of v1, /device:TPU:0, one launch (start us, length us, event | category | flops | bytes accessed | tf_op | source)
XLA Modules:
  0.0 121.4 jit_solution(6632553230254824666)
XLA Ops:
  0.7 1.0 fusion.109
  1.6 1.7 %fusion.107 = (f32[256,1,256]{2,0,1:T(8,128)S(1)}, f32[256,1,256]{2,0,1:T(8,128)}) fusion(), kind=kLoop, calls=%fused_computation.125 | loop fusion | flops 917504 | bytes 524288 | tf_op jit(solution)/shard_map/sin | solution.py:31
  3.4 1.7 %fusion.119 = (f32[1,256]{1,0:T(1,128)S(1)}, f32[1,256]{1,0:T(1,128)S(1)}, f32[1,256]{1,0:T(1,128)S(1)}, f32[1,256]{1,0:T(1,128)S(1)}, f32[1,256]{1,0:T(1,128)},...) fusion(f32[16,256]{1,0:T(8,128)} %param.8), kind=kLoop, calls=%fused_computation.155 | loop fusion | bytes 32768 | tf_op jit(solution)/shard_map/slice | solution.py:43
  5.0 3.5 %copy.105 = bf16[2,128,5888]{1,2,0:T(8,128)(2,1)S(1)} copy(bf16[2,128,5888]{2,1,0:T(8,128)(2,1)} %param.7) | data formatting | bytes 6029312 | tf_op args[0]
  8.5 1.1 maximum_bitcast_fusion.1
  9.7 7.1 %bitcast_convert_fusion = bf16[256,2,128,8]{2,0,3,1:T(8,128)(2,1)S(1)} fusion(bf16[2,128,23,256]{1,3,2,0:T(8,128)(2,1)S(1)} %bitcast.114, f32[256,1,2,256]{3,0,2,1:T(8,128)S(1)} %get-tuple-element.30, f32[256,1,2,256]{3,0,2,1:T(8,128)S(1)} %get-tuple-element.29, f32[256]{0:T(256)} %bitcast.137, f32[256]{0:T(256)} %bitcast.138, f32[256]{0:T(256)S(1)} %bitcast.124, ...), kind=kOutput, calls=%fused_computation.10 | convolution fusion | flops 3246653440 | bytes 18890752 | tf_op jit(solution)/shard_map/crsk,sitk->crit/dot_general | solution.py:46
  16.8 0.1 constant_dynamic-slice_fusion
  17.0 6.0 %collective-permute-start.6 = (bf16[32,2,128,8]{2,0,3,1:T(8,128)(2,1)S(1)}, bf16[32,2,128,8]{2,0,3,1:T(8,128)(2,1)S(1)}, u32[]{:S(2)}, u32[]{:S(2)}) collective-permute-start(bf16[32,2,128,8]{2,0,3,1:T(8,128)(2,1)S(1)} %get-tuple-element.21), channel_id=1, source_target_pairs={{0,28},{4,24},{8,20},{12,16},{16,12},{20,8},{24,4},{28,0},{1,29},{... | collective-permute-start | bytes 393224 | tf_op jit(solution)/shard_map/ppermute | solution.py:21
  23.0 0.2 collective-permute-start.5
  23.2 0.8 collective-permute-start.4
  24.0 2.0 %collective-permute-start.3 = (bf16[32,2,128,8]{2,0,3,1:T(8,128)(2,1)S(1)}, bf16[32,2,128,8]{2,0,3,1:T(8,128)(2,1)S(1)}, u32[]{:S(2)}, u32[]{:S(2)}) collective-permute-start(bf16[32,2,128,8]{2,0,3,1:T(8,128)(2,1)S(1)} %get-tuple-element.24), channel_id=1, source_target_pairs={{0,16},{4,20},{8,24},{12,28},{16,0},{20,4},{24,8},{28,12},{1,17},{... | collective-permute-start | bytes 393224 | tf_op jit(solution)/shard_map/ppermute | solution.py:21
  26.0 1.6 %collective-permute-start = (bf16[32,2,128,8]{2,0,3,1:T(8,128)(2,1)S(1)}, bf16[32,2,128,8]{2,0,3,1:T(8,128)(2,1)S(1)}, u32[]{:S(2)}, u32[]{:S(2)}) collective-permute-start(bf16[32,2,128,8]{2,0,3,1:T(8,128)(2,1)S(1)} %get-tuple-element.27), channel_id=1, source_target_pairs={{0,4},{4,0},{8,12},{12,8},{16,20},{20,16},{24,28},{28,24},{1,5},{5... | collective-permute-start | bytes 393224 | tf_op jit(solution)/shard_map/ppermute | solution.py:21
  28.1 0.1 broadcast_in_dim.22
  28.2 0.1 copy.119
  28.4 2.6 %collective-permute-done = bf16[32,2,128,8]{2,0,3,1:T(8,128)(2,1)S(1)} collective-permute-done((bf16[32,2,128,8]{2,0,3,1:T(8,128)(2,1)S(1)}, bf16[32,2,128,8]{2,0,3,1:T(8,128)(2,1)S(1)}, u32[]{:S(2)}, u32[]{:S(2)}) %collective-permute-start) | collective-permute-done | bytes 131104 | tf_op jit(solution)/shard_map/ppermute | solution.py:21
  31.0 3.5 %collective-permute-start.1 = (bf16[32,2,128,8]{2,0,3,1:T(8,128)(2,1)S(1)}, bf16[32,2,128,8]{2,0,3,1:T(8,128)(2,1)S(1)}, u32[]{:S(2)}, u32[]{:S(2)}) collective-permute-start(bf16[32,2,128,8]{2,0,3,1:T(8,128)(2,1)S(1)} %get-tuple-element.26), channel_id=1, source_target_pairs={{0,8},{4,12},{8,0},{12,4},{16,24},{20,28},{24,16},{28,20},{1,9},{5... | collective-permute-start | bytes 393224 | tf_op jit(solution)/shard_map/ppermute | solution.py:21
  34.5 2.9 %collective-permute-done.1 = bf16[32,2,128,8]{2,0,3,1:T(8,128)(2,1)S(1)} collective-permute-done((bf16[32,2,128,8]{2,0,3,1:T(8,128)(2,1)S(1)}, bf16[32,2,128,8]{2,0,3,1:T(8,128)(2,1)S(1)}, u32[]{:S(2)}, u32[]{:S(2)}) %collective-permute-start.1) | collective-permute-done | bytes 131104 | tf_op jit(solution)/shard_map/ppermute | solution.py:21
  37.4 2.9 %collective-permute-start.2 = (bf16[32,2,128,8]{2,0,3,1:T(8,128)(2,1)S(1)}, bf16[32,2,128,8]{2,0,3,1:T(8,128)(2,1)S(1)}, u32[]{:S(2)}, u32[]{:S(2)}) collective-permute-start(bf16[32,2,128,8]{2,0,3,1:T(8,128)(2,1)S(1)} %get-tuple-element.25), channel_id=1, source_target_pairs={{0,12},{4,8},{8,4},{12,0},{16,28},{20,24},{24,20},{28,16},{1,13},{... | collective-permute-start | bytes 393224 | tf_op jit(solution)/shard_map/ppermute | solution.py:21
  40.4 7.0 %collective-permute-done.2 = bf16[32,2,128,8]{2,0,3,1:T(8,128)(2,1)S(1)} collective-permute-done((bf16[32,2,128,8]{2,0,3,1:T(8,128)(2,1)S(1)}, bf16[32,2,128,8]{2,0,3,1:T(8,128)(2,1)S(1)}, u32[]{:S(2)}, u32[]{:S(2)}) %collective-permute-start.2) | collective-permute-done | bytes 131104 | tf_op jit(solution)/shard_map/ppermute | solution.py:21
  47.9 6.8 %fusion.58 = f32[32,2,2,64,2]{3,4,1,2,0:T(2,128)S(1)} fusion(bf16[32,2,1024,8]{2,3,1,0:T(8,128)(2,1)S(1)} %copy_dynamic-update-slice_fusion, s32[]{:T(128)S(6)} %select_n.103, bf16[2,32,64,1024]{3,2,1,0:T(8,128)(2,1)} %param.9, bf16[64,1024]{1,0:T(8,128)(2,1)S(1)} %copy.119), kind=kOutput, calls=%fused_computation.64 | convolution fusion | flops 37748736 | bytes 8847364 | tf_op jit(solution)/shard_map/scbi,crit->csrbt/dot_general | solution.py:75
  55.0 0.7 reshape.186
  55.7 3.4 %all-to-all-start = ((bf16[4,2,1024]{2,1,0:T(2,128)(2,1)}), bf16[4,2,1024]{2,1,0:T(2,128)(2,1)S(1)}, u32[]{:S(2)}, u32[]{:S(2)}) async-start(bf16[4,2,1024]{2,1,0:T(2,128)(2,1)} %reshape.186), calls=%async_computation | async-start | bytes 32768 | tf_op jit(solution)/shard_map/all_to_all | solution.py:94
  59.1 1.0 gather_fusion.1
  60.1 1.2 %fusion.97 = (bf16[1,32,2,9,128,8]{4,5,2,0,3,1:T(8,128)(2,1)}, bf16[32,2,9,128,8]{3,4,1,2,0:T(8,128)(2,1)S(1)}) fusion(bf16[9,32,2,128,8]{3,4,2,1,0:T(8,128)(2,1)S(1)} %gather_fusion.1, pred[9]{0:T(512)(128)(4,1)S(1)} %get-tuple-element.47), kind=kLoop, calls=%fused_computation.107 | loop fusion | flops 589824 | bytes 3538953 | tf_op jit(solution)/shard_map/stack | solution.py:64
  61.4 0.2 fusion.118
  61.5 0.2 maximum_bitcast_fusion
  61.7 1.0 gather_fusion
  62.9 0.7 reshape.188
  63.7 4.0 %all-to-all-start.1 = ((bf16[8,2,512]{2,1,0:T(2,128)(2,1)}), bf16[8,2,512]{2,1,0:T(2,128)(2,1)S(1)}, u32[]{:S(2)}, u32[]{:S(2)}) async-start(bf16[8,2,512]{2,1,0:T(2,128)(2,1)} %reshape.188), calls=%async_computation.1 | async-start | bytes 32768 | tf_op jit(solution)/shard_map/all_to_all | solution.py:93
  67.6 16.0 %fusion = f32[2,32,9,128,128]{3,4,0,2,1:T(8,128)} fusion(bf16[1,32,2,9,128,8]{4,5,2,0,3,1:T(8,128)(2,1)S(1)} %maximum_bitcast_fusion, bf16[1,32,2,9,128,8]{4,5,2,0,3,1:T(8,128)(2,1)} %get-tuple-element.17, bf16[9,32,2,128,8]{3,4,2,1,0:T(8,128)(2,1)S(1)} %gather_fusion, pred[9]{0:T(512)(128)(4,1)S(1)} %get-tuple-element.13), kind=kOutput, calls=%fused_computation.3 | convolution fusion | flops 316735488 | bytes 41287688 | tf_op jit(solution)/shard_map/ocrkaw,crkbw->ockab/dot_general | solution.py:65
  83.6 36.9 %copy.128 = f32[2,32,9,128,128]{4,3,2,1,0:T(8,128)} copy(f32[2,32,9,128,128]{3,4,0,2,1:T(8,128)} %fusion) | data formatting | bytes 75497472
  120.6 0.7 all_to_all.27
  (33 shorter events, 1.5 us)
Async XLA Ops:
  16.8 11.0 %copy-start.1 = (s32[9,2]{0,1:T(2,128)S(1)}, s32[9,2]{0,1:T(2,128)}, u32[]{:S(2)}) copy-start(s32[9,2]{0,1:T(2,128)} %param.11) | copy-start | bytes 220
  16.8 11.1 %copy-start = (s32[64,512]{1,0:T(8,128)S(1)}, s32[64,512]{1,0:T(8,128)}, u32[]{:S(2)}) copy-start(s32[64,512]{1,0:T(8,128)} %param.10) | copy-start | bytes 393220
  17.0 30.8 %collective-permute-start.6 = (bf16[32,2,128,8]{2,0,3,1:T(8,128)(2,1)S(1)}, bf16[32,2,128,8]{2,0,3,1:T(8,128)(2,1)S(1)}, u32[]{:S(2)}, u32[]{:S(2)}) collective-permute-start(bf16[32,2,128,8]{2,0,3,1:T(8,128)(2,1)S(1)} %get-tuple-element.21), channel_id=1, source_target_pairs={{0,28},{4,24},{8,20},{12,16},{16,12},{20,8},{24,4},{28,0},{1,29},{... | collective-permute-start | bytes 393224 | tf_op jit(solution)/shard_map/ppermute | solution.py:21
  23.0 24.7 %collective-permute-start.5 = (bf16[32,2,128,8]{2,0,3,1:T(8,128)(2,1)S(1)}, bf16[32,2,128,8]{2,0,3,1:T(8,128)(2,1)S(1)}, u32[]{:S(2)}, u32[]{:S(2)}) collective-permute-start(bf16[32,2,128,8]{2,0,3,1:T(8,128)(2,1)S(1)} %get-tuple-element.22), channel_id=1, source_target_pairs={{0,24},{4,28},{8,16},{12,20},{16,8},{20,12},{24,0},{28,4},{1,25},{... | collective-permute-start | bytes 393224 | tf_op jit(solution)/shard_map/ppermute | solution.py:21
  23.2 24.4 %collective-permute-start.4 = (bf16[32,2,128,8]{2,0,3,1:T(8,128)(2,1)S(1)}, bf16[32,2,128,8]{2,0,3,1:T(8,128)(2,1)S(1)}, u32[]{:S(2)}, u32[]{:S(2)}) collective-permute-start(bf16[32,2,128,8]{2,0,3,1:T(8,128)(2,1)S(1)} %get-tuple-element.23), channel_id=1, source_target_pairs={{0,20},{4,16},{8,28},{12,24},{16,4},{20,0},{24,12},{28,8},{1,21},{... | collective-permute-start | bytes 393224 | tf_op jit(solution)/shard_map/ppermute | solution.py:21
  24.0 23.5 %collective-permute-start.3 = (bf16[32,2,128,8]{2,0,3,1:T(8,128)(2,1)S(1)}, bf16[32,2,128,8]{2,0,3,1:T(8,128)(2,1)S(1)}, u32[]{:S(2)}, u32[]{:S(2)}) collective-permute-start(bf16[32,2,128,8]{2,0,3,1:T(8,128)(2,1)S(1)} %get-tuple-element.24), channel_id=1, source_target_pairs={{0,16},{4,20},{8,24},{12,28},{16,0},{20,4},{24,8},{28,12},{1,17},{... | collective-permute-start | bytes 393224 | tf_op jit(solution)/shard_map/ppermute | solution.py:21
  26.0 5.0 %collective-permute-start = (bf16[32,2,128,8]{2,0,3,1:T(8,128)(2,1)S(1)}, bf16[32,2,128,8]{2,0,3,1:T(8,128)(2,1)S(1)}, u32[]{:S(2)}, u32[]{:S(2)}) collective-permute-start(bf16[32,2,128,8]{2,0,3,1:T(8,128)(2,1)S(1)} %get-tuple-element.27), channel_id=1, source_target_pairs={{0,4},{4,0},{8,12},{12,8},{16,20},{20,16},{24,28},{28,24},{1,5},{5... | collective-permute-start | bytes 393224 | tf_op jit(solution)/shard_map/ppermute | solution.py:21
  31.0 6.4 %collective-permute-start.1 = (bf16[32,2,128,8]{2,0,3,1:T(8,128)(2,1)S(1)}, bf16[32,2,128,8]{2,0,3,1:T(8,128)(2,1)S(1)}, u32[]{:S(2)}, u32[]{:S(2)}) collective-permute-start(bf16[32,2,128,8]{2,0,3,1:T(8,128)(2,1)S(1)} %get-tuple-element.26), channel_id=1, source_target_pairs={{0,8},{4,12},{8,0},{12,4},{16,24},{20,28},{24,16},{28,20},{1,9},{5... | collective-permute-start | bytes 393224 | tf_op jit(solution)/shard_map/ppermute | solution.py:21
  37.4 10.0 %collective-permute-start.2 = (bf16[32,2,128,8]{2,0,3,1:T(8,128)(2,1)S(1)}, bf16[32,2,128,8]{2,0,3,1:T(8,128)(2,1)S(1)}, u32[]{:S(2)}, u32[]{:S(2)}) collective-permute-start(bf16[32,2,128,8]{2,0,3,1:T(8,128)(2,1)S(1)} %get-tuple-element.25), channel_id=1, source_target_pairs={{0,12},{4,8},{8,4},{12,0},{16,28},{20,24},{24,20},{28,16},{1,13},{... | collective-permute-start | bytes 393224 | tf_op jit(solution)/shard_map/ppermute | solution.py:21
  55.7 7.1 %all-to-all-start = ((bf16[4,2,1024]{2,1,0:T(2,128)(2,1)}), bf16[4,2,1024]{2,1,0:T(2,128)(2,1)S(1)}, u32[]{:S(2)}, u32[]{:S(2)}) async-start(bf16[4,2,1024]{2,1,0:T(2,128)(2,1)} %reshape.186), calls=%async_computation | async-start | bytes 32768 | tf_op jit(solution)/shard_map/all_to_all | solution.py:94
  63.7 56.8 %all-to-all-start.1 = ((bf16[8,2,512]{2,1,0:T(2,128)(2,1)}), bf16[8,2,512]{2,1,0:T(2,128)(2,1)S(1)}, u32[]{:S(2)}, u32[]{:S(2)}) async-start(bf16[8,2,512]{2,1,0:T(2,128)(2,1)} %reshape.188), calls=%async_computation.1 | async-start | bytes 32768 | tf_op jit(solution)/shard_map/all_to_all | solution.py:93
